TPU v7x, 1024 devices: a whole 4x4x32 slice. The times are simulated.
1024 devices in a mesh: dp: 64 (over z, core), etp: 16 (over x, y).
Axes of the slice: x: 4, y: 4, z: 32, core: 2. Of those that a mesh axis runs over, the one named last changes fastest.
Arguments:
- tokens: bfloat16 [1024, 3072], P('dp', 'etp'), may hold values from -6 to 6
- upstream: bfloat16 [1024, 3072], P('dp', 'etp'), may hold values from -6 to 6
- route_ids: int32 [1024, 2], P('dp'), may hold values from 0 to 7, all different within a row; in each aligned block of 16 rows (0 to 15, 16 to 31, ...) at most 8 rows name the same one
- route_weights: float32 [1024, 2], P('dp'), may hold values from 0.1 to 1
- w_gate: bfloat16 [3072, 131072], P(None, ('dp', 'etp')), may hold values from -0.109375 to 0.109375
- w_up: bfloat16 [3072, 131072], P(None, ('dp', 'etp')), may hold values from -0.109375 to 0.109375
- w_down: bfloat16 [131072, 3072], P(('dp', 'etp')), may hold values from -0.046875 to 0.046875
Outputs:
- grad_tokens: float32 [1024, 3072], P('dp', 'etp')
Inputs may be any that keep to these rules, and one draw needn't show every extreme that they name: `route_ids`: among the 16 tokens of one index of dp no expert is named by more than 8 tokens; in some of them one expert is named by exactly 8.
All inputs are finite; a program needn't handle non-finite values.
Results may differ from a plain program's by a relative error of at most 0.004.
Values may be sent and summed in bfloat16 or wider, within the bound.
A program may use at most 64 MiB of HBM per device.

v0:
```python
import jax
import jax.numpy as jnp
from jax import lax
from jax.sharding import PartitionSpec as P

EXPERTS = 8


def local(tokens, upstream, route_ids, route_weights, w_gate, w_up, w_down):
    tok_rows = tokens.shape[0]
    capacity = tok_rows // 2
    devices_dp = lax.axis_size("dp")
    group_size = devices_dp // EXPERTS
    picks = (route_ids[:, :, None] == jnp.arange(EXPERTS, dtype=jnp.int32)[None, None, :]).astype(
        jnp.int32
    )
    hit_count = jnp.sum(picks, axis=1)
    before = jnp.cumsum(hit_count, axis=0) - hit_count
    slot_of = jnp.sum(picks * before[:, None, :], axis=2)
    target = (route_ids * capacity + slot_of).reshape(-1)
    placing = (target[:, None] == jnp.arange(EXPERTS * capacity, dtype=jnp.int32)[None, :]).astype(
        jnp.float32
    )
    placing_half = placing.astype(jnp.bfloat16)
    scaled = (route_weights[:, :, None] * upstream[:, None, :].astype(jnp.float32)).astype(
        jnp.bfloat16
    )
    scaled = scaled.reshape(2 * tok_rows, -1)
    doubled = jnp.broadcast_to(tokens[:, None, :], (tok_rows, 2, tokens.shape[1])).reshape(
        2 * tok_rows, -1
    )

    def to_slots(rows):
        slot_rows = lax.dot_general(
            placing_half, rows, (((0,), (0,)), ((), ())), preferred_element_type=jnp.float32
        ).astype(jnp.bfloat16)
        spread = jnp.broadcast_to(
            slot_rows.reshape(EXPERTS, 1, capacity, -1),
            (EXPERTS, group_size, capacity, slot_rows.shape[1]),
        )
        return spread.reshape(devices_dp, capacity, -1)

    got_x, got_dy = (
        lax.all_to_all(to_slots(doubled), "dp", split_axis=0, concat_axis=0, tiled=True),
        lax.all_to_all(to_slots(scaled), "dp", split_axis=0, concat_axis=0, tiled=True),
    )
    flat_x = got_x.reshape(devices_dp * capacity, -1)
    flat_dy = got_dy.reshape(devices_dp * capacity, -1)
    full_x, full_dy = (
        lax.all_gather(flat_x, "etp", axis=1, tiled=True),
        lax.all_gather(flat_dy, "etp", axis=1, tiled=True),
    )
    gate_pre = jnp.dot(full_x, w_gate, preferred_element_type=jnp.float32)
    up_pre = jnp.dot(full_x, w_up, preferred_element_type=jnp.float32)
    back_grad = lax.dot_general(
        full_dy, w_down, (((1,), (1,)), ((), ())), preferred_element_type=jnp.float32
    )
    sigmoid_gate = jax.nn.sigmoid(gate_pre)
    d_gate = (back_grad * up_pre * sigmoid_gate * (1.0 + gate_pre * (1.0 - sigmoid_gate))).astype(
        jnp.bfloat16
    )
    d_up = (back_grad * gate_pre * sigmoid_gate).astype(jnp.bfloat16)
    term = lax.dot_general(
        w_gate, d_gate, (((1,), (1,)), ((), ())), preferred_element_type=jnp.float32
    )
    own_rows = lax.psum_scatter(
        term
        + lax.dot_general(w_up, d_up, (((1,), (1,)), ((), ())), preferred_element_type=jnp.float32),
        "etp",
        scatter_dimension=0,
        tiled=True,
    )
    returned = jnp.transpose(own_rows).reshape(devices_dp, capacity, -1)
    came_back = lax.all_to_all(returned, "dp", split_axis=0, concat_axis=0, tiled=True)
    summed = jnp.sum(came_back.reshape(EXPERTS, group_size, capacity, -1), axis=1).reshape(
        EXPERTS * capacity, -1
    )
    per_route = jnp.dot(placing, summed, precision=lax.Precision.HIGHEST)
    return jnp.sum(per_route.reshape(tok_rows, 2, -1), axis=1)


def solution(mesh):
    in_specs = (
        P("dp", "etp"),
        P("dp", "etp"),
        P("dp", None),
        P("dp", None),
        P(None, ("dp", "etp")),
        P(None, ("dp", "etp")),
        P(("dp", "etp"), None),
    )
    out_specs = P("dp", "etp")
    return jax.shard_map(local, mesh=mesh, in_specs=in_specs, out_specs=out_specs, check_vma=False)
```

profile of v0, /device:TPU:6, one launch (start us, length us, event | category | flops | bytes accessed | tf_op | source)
XLA Modules:
  0.0 474.3 jit_solution(9557693391156804331)
XLA Ops:
  6.5 0.0 copy-start
  6.5 0.0 copy-start.2
  6.5 0.0 all-gather.3.cloned.1.call-start
  6.5 0.8 convert_reduce_fusion
  7.3 0.1 copy.24
  7.5 0.1 copy.26
  7.5 0.7 select_reduce_fusion
  8.2 0.7 multiply_add_fusion
  8.9 0.1 copy.27
  9.0 0.1 eq.57
  9.1 0.8 copy.28
  9.9 0.1 mul.54
  9.9 0.7 mul.56
  10.7 0.2 fusion.4
  11.0 72.2 %all_to_all.15 = bf16[64,8,192]{2,1,0:T(8,128)(2,1)S(1)} all-to-all(bf16[64,8,192]{2,1,0:T(8,128)(2,1)S(1)} %bitcast.36), channel_id=1, replica_groups=mesh['dp'=64,'etp'=16] {'dp'}, dimensions={0} | all-to-all | bytes 393216 | tf_op jit(solution)/shard_map/all_to_all | solution.py:45
  83.2 0.0 copy-start.1
  83.2 0.8 copy.29
  84.0 0.0 all-gather.3.cloned.1.call-update
  84.0 0.0 all-gather.5.cloned.1.call-start
  84.0 0.7 broadcast_in_dim.12
  84.8 0.2 fusion.5
  85.1 47.1 %all_to_all.16 = bf16[64,8,192]{2,1,0:T(8,128)(2,1)S(1)} all-to-all(bf16[64,8,192]{2,1,0:T(8,128)(2,1)S(1)} %bitcast.37), channel_id=1, replica_groups=mesh['dp'=64,'etp'=16] {'dp'}, dimensions={0} | all-to-all | bytes 393216 | tf_op jit(solution)/shard_map/all_to_all | solution.py:44
  132.2 0.8 copy.30
  133.0 0.0 all-gather.5.cloned.1.call-update
  133.0 0.0 reduce-scatter.4.cloned.1.call-start
  133.0 15.4 %all-gather.3.cloned.1.call-done = bf16[512,3072]{0,1:T(8,128)(2,1)} async-done(((bf16[512,192]{0,1:T(8,128)(2,1)}), bf16[512,3072]{0,1:T(8,128)(2,1)}) %all-gather.3.cloned.1.call-update) | async-done | bytes 3145744 | tf_op jit(solution)/shard_map/all_gather | solution.py:51
  148.4 0.0 copy-done.2
  148.4 2.9 fusion.20
  151.3 84.3 %all-gather.5.cloned.1.call-done = bf16[512,3072]{0,1:T(8,128)(2,1)} async-done(((bf16[512,192]{0,1:T(8,128)(2,1)}), bf16[512,3072]{0,1:T(8,128)(2,1)}) %all-gather.5.cloned.1.call-update) | async-done | bytes 3145744 | tf_op jit(solution)/shard_map/all_gather | solution.py:50
  235.7 0.0 copy-done.1
  235.7 2.9 fusion.21
  238.6 0.0 copy-done
  238.6 8.0 %fusion.3 = f32[512,3072]{1,0:T(8,128)} fusion(bf16[3072,128]{1,0:T(8,128)(2,1)S(1)} %copy-done.1, f32[512,128]{1,0:T(8,128)S(1)} %fusion.20, bf16[512,3072]{0,1:T(8,128)(2,1)} %all-gather.5.cloned.1.call-done, bf16[3072,128]{1,0:T(8,128)(2,1)S(1)} %copy-done, f32[512,128]{1,0:T(8,128)S(1)} %fusion.21), kind=kOutput, calls=%fused_computation.5 | convolution fusion | flops 805961728 | bytes 11534336 | tf_op jit(solution)/shard_map/dot_general | solution.py:63
  246.5 6.4 %add_bitcast_fusion = f32[3072,512]{0,1:T(8,128)} fusion(f32[512,3072]{1,0:T(8,128)} %fusion.3, bf16[3072,128]{1,0:T(8,128)(2,1)S(1)} %copy-done, f32[512,128]{1,0:T(8,128)S(1)} %fusion.20, f32[512,128]{1,0:T(8,128)S(1)} %fusion.21), kind=kOutput, calls=%fused_computation | convolution fusion | flops 404619264 | bytes 13893632 | tf_op jit(solution)/shard_map/dot_general | solution.py:68
  253.0 6.6 %copy.31 = f32[3072,512]{1,0:T(8,128)} copy(f32[3072,512]{0,1:T(8,128)} %add_bitcast_fusion) | data formatting | bytes 12582912
  259.6 0.0 reduce-scatter.4.cloned.1.call-update
  259.6 117.0 %reduce-scatter.4.cloned.1.call-done = f32[192,512]{1,0:T(8,128)} async-done(((f32[3072,512]{1,0:T(8,128)}), f32[192,512]{1,0:T(8,128)}) %reduce-scatter.4.cloned.1.call-update) | async-done | bytes 393232
  376.6 1.2 copy.32
  377.8 89.1 %all_to_all.17 = f32[64,8,192]{2,1,0:T(8,128)S(1)} all-to-all(f32[64,8,192]{2,1,0:T(8,128)S(1)} %bitcast.33), channel_id=1, replica_groups=mesh['dp'=64,'etp'=16] {'dp'}, dimensions={0} | all-to-all | bytes 786432 | tf_op jit(solution)/shard_map/all_to_all | solution.py:74
  466.9 0.8 convolution_reduce_fusion
  (7 shorter events, 0.2 us)
Async XLA Ops:
  6.5 232.0 %copy-start = (bf16[3072,128]{1,0:T(8,128)(2,1)S(1)}, bf16[3072,128]{1,0:T(8,128)(2,1)}, u32[]{:S(2)}) copy-start(bf16[3072,128]{1,0:T(8,128)(2,1)} %param.12) | copy-start | bytes 2359300
  6.5 141.9 %copy-start.2 = (bf16[128,3072]{1,0:T(8,128)(2,1)S(1)}, bf16[128,3072]{1,0:T(8,128)(2,1)}, u32[]{:S(2)}) copy-start(bf16[128,3072]{1,0:T(8,128)(2,1)} %param.13) | copy-start | bytes 2359300
  6.5 141.9 %all-gather.3.cloned.1.call-start = ((), (), s32[]{:S(2)}) async-start(), calls=%async_computation.4 | async-start | bytes 3342336 | tf_op jit(solution)/shard_map/all_gather | solution.py:51
  83.2 152.5 %copy-start.1 = (bf16[3072,128]{1,0:T(8,128)(2,1)S(1)}, bf16[3072,128]{1,0:T(8,128)(2,1)}, u32[]{:S(2)}) copy-start(bf16[3072,128]{1,0:T(8,128)(2,1)} %param.11) | copy-start | bytes 2359300
  84.0 151.7 %all-gather.5.cloned.1.call-start = ((), (), s32[]{:S(2)}) async-start(), calls=%async_computation.5 | async-start | bytes 3342336 | tf_op jit(solution)/shard_map/all_gather | solution.py:50
  133.0 243.6 %reduce-scatter.4.cloned.1.call-start = ((), (), s32[]{:S(2)}) async-start(), calls=%async_computation.6 | async-start | bytes 6684672
Sparse Core Ops, SparseCore 0:
  84.1 64.2 all-gather.2
  152.6 82.9 all-gather.4
  259.7 116.8 reduce-scatter.3
where the time goes:
time: 475 us; the launch traced here: 474 us
  waiting for transfers between devices  217 us (46%)
  blocking collectives  208 us (44%)
  matrix products  21.5 us (5%)
  between operations  13.2 us (3%)
  local copies, waits for them, and re-layouts  12.1 us (3%)
    unnamed x4, waiting for transfers between devices  117 us
    all_to_all x1, blocking collectives, local(): lax.all_to_all(returned, 'dp', split_axis=0, concat_axis=0, tiled=True)  89.1 us
    all_gather x1, waiting for transfers between devices, local(): lax.all_gather(flat_x, 'etp', axis=1, tiled=True)  84.3 us
    all_to_all x1, blocking collectives, local(): lax.all_to_all(to_slots(scaled), 'dp', split_axis=0, concat_axis=0, tiled...  72.2 us
    all_to_all x1, blocking collectives, local(): lax.all_to_all(to_slots(doubled), 'dp', split_axis=0, concat_axis=0, tile...  47.1 us
    all_gather x1, waiting for transfers between devices, local(): lax.all_gather(flat_dy, 'etp', axis=1, tiled=True)  15.4 us
  transfers between devices with their start and end apart: 3, of which 3 were waited for; matrix products, arithmetic and copies ran while one was open for 1% of the time, Pallas kernels for 0%

commit v1 on v0

v1 whole, which is shorter than its diff:
```python
import functools

import jax
import jax.numpy as jnp
from jax import lax
from jax.experimental import pallas as pl
from jax.experimental.pallas import tpu as pltpu
from jax.sharding import PartitionSpec as P

EXPERTS = 8
CORES = 2
RING = 4
WIN = 256
F32 = jnp.float32
BF16 = jnp.bfloat16
MESH = pl.DeviceIdType.MESH


def nn(a, b, precision=None):
    return lax.dot_general(a, b, (((1,), (0,)), ((), ())), preferred_element_type=F32, precision=precision)


def nt(a, b):
    return lax.dot_general(a, b, (((1,), (1,)), ((), ())), preferred_element_type=F32)


def tn(a, b):
    return lax.dot_general(a, b, (((0,), (0,)), ((), ())), preferred_element_type=F32)


def kernel(
    zl_n,
    tok_ref, up_ref, ids_ref, rw_ref, wg_hbm, wu_hbm, wd_hbm,
    out_ref,
    wg, wu, wd, blk, zbuf, zfull, dgu, sbuf, relay, main, tsum, thalf, relay2, main2, fsum, fhalf, zrecv, vsum, rfin,
    load_sem, send_sem, recv_sem,
):
    src_n = zl_n * EXPERTS
    half_src = src_n // 2
    tok, feat = tok_ref.shape
    cap = tok // 2
    dp, etp = lax.axis_index("dp"), lax.axis_index("etp")
    core, z = dp % CORES, dp // CORES
    zl, e = z % zl_n, z // zl_n
    x, y = etp // RING, etp % RING
    odd = etp % 2
    counter = [0]
    started = []

    def at_dp(zz, cc):
        return {"dp": zz * CORES + cc}

    def at_xy(xx, yy):
        return {"etp": xx * RING + yy}

    def send(src, dst, device):
        k = counter[0]
        counter[0] += 1
        cp = pltpu.make_async_remote_copy(
            src_ref=src, dst_ref=dst, send_sem=send_sem.at[k], recv_sem=recv_sem.at[k], device_id=device,
            device_id_type=MESH,
        )
        cp.start()
        started.append(cp)
        return cp

    hid = wg_hbm.shape[1]
    loads = [
        pltpu.make_async_copy(wg_hbm, wg.at[:, 0:hid], load_sem.at[0]),
        pltpu.make_async_copy(wu_hbm, wu.at[:, 0:hid], load_sem.at[1]),
        pltpu.make_async_copy(wd_hbm, wd.at[0:hid, :], load_sem.at[2]),
    ]
    for cp in loads:
        cp.start()

    partners = [at_dp(z, 1 - core)]
    partners += [at_dp((e + d) % EXPERTS * zl_n + zl, core) for d in range(1, EXPERTS)]
    partners += [at_dp(e * zl_n + (zl + d) % zl_n, core) for d in range(1, zl_n)]
    partners += [at_xy((x + d) % RING, y) for d in (1, RING - 1)]
    partners += [at_xy(x, (y + d) % RING) for d in (1, RING - 1)]
    barrier = pltpu.get_barrier_semaphore()
    for device in partners:
        pl.semaphore_signal(barrier, inc=1, device_id=device, device_id_type=MESH)

    lane = lax.broadcasted_iota(jnp.int32, (tok, EXPERTS * cap), 1)
    lane_e, lane_s = lane >> 3, lane & 7
    ids = ids_ref[...]
    hit0, hit1 = ids[:, 0:1] == lane_e, ids[:, 1:2] == lane_e
    one0, one1 = jnp.where(hit0, 1.0, 0.0).astype(F32), jnp.where(hit1, 1.0, 0.0).astype(F32)
    lower = lax.broadcasted_iota(jnp.int32, (tok, tok), 1) < lax.broadcasted_iota(jnp.int32, (tok, tok), 0)
    before = nn(jnp.where(lower, 1.0, 0.0).astype(F32), one0 + one1)
    slot_ok = jnp.where(before == lane_s.astype(F32), 1.0, 0.0).astype(F32)
    p0, p1 = one0 * slot_ok, one1 * slot_ok
    placed = p0 + p1
    shift = lax.broadcasted_iota(jnp.int32, (feat, WIN), 1) - lax.broadcasted_iota(jnp.int32, (feat, WIN), 0)
    spread = jnp.where(shift == odd * (WIN - feat), 1.0, 0.0).astype(BF16)
    xw = nn(tok_ref[...], spread).astype(BF16)
    uw = nn(up_ref[...], spread)
    rw = rw_ref[...]
    d0, d1 = (rw[:, 0:1] * uw).astype(BF16), (rw[:, 1:2] * uw).astype(BF16)
    xs = tn(placed.astype(BF16), xw).reshape(EXPERTS, cap, WIN)
    ds = (tn(p0.astype(BF16), d0) + tn(p1.astype(BF16), d1)).reshape(EXPERTS, cap, WIN)
    blk[...] = jnp.concatenate([xs, ds], axis=1).astype(BF16)

    pl.semaphore_wait(barrier, len(partners))

    half = zl // (zl_n // 2)
    pa, pb = x + half * (y - x), y + half * (x - y)
    zrow = pl.multiple_of(zl % (zl_n // 2) * (EXPERTS * tok), EXPERTS * tok)
    mine = zbuf.at[half, pa, pb, pl.ds(pl.multiple_of(zrow + e * tok, tok), tok)]
    own = pltpu.make_async_copy(blk.at[e], mine, load_sem.at[3])
    own.start()
    moves = []
    for d in range(1, EXPERTS):
        to = (e + d) % EXPERTS
        moves.append(send(blk.at[to], mine, at_dp(to * zl_n + zl, core)))
    sibling = at_dp(z, 1 - core)
    weights = [
        send(wd_hbm, wd.at[hid:, :], sibling),
        send(wg_hbm, wg.at[:, hid:], sibling),
        send(wu_hbm, wu.at[:, hid:], sibling),
    ]
    own.wait()
    for cp in moves:
        cp.wait_recv()
    region = zbuf.at[half, pa, pb, pl.ds(zrow, EXPERTS * tok)]
    moves = [send(region, region, at_dp(e * zl_n + (zl + d) % zl_n, core)) for d in range(1, zl_n)]
    for cp in moves:
        cp.wait_recv()

    def ahead(h, stage, step):
        if (h == 0) == (stage == 0):
            return at_xy((x + step) % RING, y)
        return at_xy(x, (y + step) % RING)

    def place(h):
        return (x, y) if h == 0 else (y, x)

    rows = half_src * tok
    lo, hi = slice(0, rows // 2), slice(rows // 2, rows)

    def block(h, stage, step, part):
        a, b = place(h)
        if stage == 0:
            return zbuf.at[h, (a + step + RING) % RING, b, part]
        return zbuf.at[h, :, (b + step + RING) % RING, part]

    for stage in range(2):
        first = []
        for h in range(2):
            first.append([
                send(block(h, stage, 0, lo), block(h, stage, 0, lo), ahead(h, stage, 1)),
                send(block(h, stage, 0, hi), block(h, stage, 0, hi), ahead(h, stage, RING - 1)),
                send(block(h, stage, 0, hi), block(h, stage, 0, hi), ahead(h, stage, 1)),
                send(block(h, stage, 0, lo), block(h, stage, 0, lo), ahead(h, stage, RING - 1)),
            ])
        second = []
        for h in range(2):
            first[h][0].wait_recv()
            second.append(send(block(h, stage, -1, lo), block(h, stage, -1, lo), ahead(h, stage, 1)))
            first[h][1].wait_recv()
            second.append(send(block(h, stage, 1, hi), block(h, stage, 1, hi), ahead(h, stage, RING - 1)))
        for h in range(2):
            first[h][2].wait_recv()
            first[h][3].wait_recv()
        for cp in second:
            cp.wait_recv()

    for cp in loads:
        cp.wait()
    for cp in weights:
        cp.wait_recv()

    pairs = RING * RING // 2
    lanes = 2 * feat

    def pair_place(h, j):
        px, py = j // (RING // 2), j % (RING // 2) * 2
        return ((px, py), (px, py + 1)) if h == 0 else ((py, px), (py + 1, px))

    slots = half_src * cap
    for h in range(2):
        for j in range(pairs):
            (a0, b0), (a1, b1) = pair_place(h, j)
            row = slice(h * rows, (h + 1) * rows)
            base = j * lanes
            zfull[row, base:base + 128] = zbuf[h, a0, b0, :, 0:128]
            zfull[row, base + 128:base + 256] = zbuf[h, a0, b0, :, 128:256] + zbuf[h, a1, b1, :, 0:128]
            zfull[row, base + 256:base + 384] = zbuf[h, a1, b1, :, 128:256]

    chip_hid = CORES * hid
    for h in range(2):
        act = zfull[h * rows:(h + 1) * rows, :]
        gate = nn(act, wg[...]).reshape(half_src, tok, chip_hid)[:, 0:cap].reshape(slots, chip_hid)
        up = nn(act, wu[...]).reshape(half_src, tok, chip_hid)[:, 0:cap].reshape(slots, chip_hid)
        back = nt(act, wd[...]).reshape(half_src, tok, chip_hid)[:, cap:tok].reshape(slots, chip_hid)
        sig = 1.0 / (1.0 + jnp.exp(-gate))
        dgu[h * slots:(h + 1) * slots, 0:chip_hid] = (back * up * sig * (1.0 + gate * (1.0 - sig))).astype(BF16)
        dgu[h * slots:(h + 1) * slots, chip_hid:] = (back * gate * sig).astype(BF16)
    for j in range(pairs):
        part = nt(dgu[:, 0:chip_hid], wg[j * lanes:(j + 1) * lanes, :])
        part = part + nt(dgu[:, chip_hid:], wu[j * lanes:(j + 1) * lanes, :])
        part = part.astype(BF16)
        for h in range(2):
            (a0, b0), (a1, b1) = pair_place(h, j)
            sbuf[h, a0, b0] = part[h * slots:(h + 1) * slots, 0:256]
            sbuf[h, a1, b1] = part[h * slots:(h + 1) * slots, 128:384]

    slo, shi = slice(0, slots // 2), slice(slots // 2, slots)

    def add(a, b):
        return a.astype(F32) + b.astype(F32)

    first = []
    for h in range(2):
        a = place(h)[0]
        nxt, opp, prv = (a + 1) % RING, (a + 2) % RING, (a + 3) % RING
        first.append([
            send(sbuf.at[h, opp, :, slo], relay.at[h, 0], ahead(h, 0, 1)),
            send(sbuf.at[h, opp, :, shi], relay.at[h, 1], ahead(h, 0, RING - 1)),
            send(sbuf.at[h, nxt, :, shi], main.at[h, 0, :, shi], ahead(h, 0, 1)),
            send(sbuf.at[h, prv, :, slo], main.at[h, 1, :, slo], ahead(h, 0, RING - 1)),
        ])
    second = []
    for h in range(2):
        a = place(h)[0]
        nxt, prv = (a + 1) % RING, (a + 3) % RING
        first[h][0].wait_recv()
        sbuf[h, nxt, :, slo] = add(sbuf[h, nxt, :, slo], relay[h, 0]).astype(BF16)
        first[h].append(send(sbuf.at[h, nxt, :, slo], main.at[h, 0, :, slo], ahead(h, 0, 1)))
        first[h][1].wait_recv()
        sbuf[h, prv, :, shi] = add(sbuf[h, prv, :, shi], relay[h, 1]).astype(BF16)
        first[h].append(send(sbuf.at[h, prv, :, shi], main.at[h, 1, :, shi], ahead(h, 0, RING - 1)))
    second = []
    for h in range(2):
        for cp in first[h][2:]:
            cp.wait_recv()
        a, b = place(h)
        total = add(sbuf[h, a], main[h, 0]) + main[h, 1].astype(F32)
        tsum[h] = total
        thalf[h] = total.astype(BF16)
        nxt, opp, prv = (b + 1) % RING, (b + 2) % RING, (b + 3) % RING
        second.append([
            send(thalf.at[h, opp, slo], relay2.at[h, 0], ahead(h, 1, 1)),
            send(thalf.at[h, opp, shi], relay2.at[h, 1], ahead(h, 1, RING - 1)),
            send(thalf.at[h, nxt, shi], main2.at[h, 0, shi], ahead(h, 1, 1)),
            send(thalf.at[h, prv, slo], main2.at[h, 1, slo], ahead(h, 1, RING - 1)),
        ])
    for h in range(2):
        b = place(h)[1]
        nxt, prv = (b + 1) % RING, (b + 3) % RING
        second[h][0].wait_recv()
        thalf[h, nxt, slo] = (tsum[h, nxt, slo] + relay2[h, 0].astype(F32)).astype(BF16)
        second[h].append(send(thalf.at[h, nxt, slo], main2.at[h, 0, slo], ahead(h, 1, 1)))
        second[h][1].wait_recv()
        thalf[h, prv, shi] = (tsum[h, prv, shi] + relay2[h, 1].astype(F32)).astype(BF16)
        second[h].append(send(thalf.at[h, prv, shi], main2.at[h, 1, shi], ahead(h, 1, RING - 1)))
    per_zl = EXPERTS * cap
    for h in range(2):
        for cp in second[h][2:]:
            cp.wait_recv()
        b = place(h)[1]
        total = tsum[h, b] + main2[h, 0].astype(F32) + main2[h, 1].astype(F32)
        total = total.reshape(zl_n // 2, per_zl, WIN)
        fsum[h * (zl_n // 2):(h + 1) * (zl_n // 2)] = total
        fhalf[h * (zl_n // 2):(h + 1) * (zl_n // 2)] = total.astype(BF16)

    moves = []
    for d in range(1, zl_n):
        to = (zl + d) % zl_n
        moves.append(send(fhalf.at[to], zrecv.at[d - 1], at_dp(e * zl_n + to, core)))
    for cp in moves:
        cp.wait_recv()
    total = fsum[zl]
    for d in range(1, zl_n):
        total = total + zrecv[d - 1].astype(F32)
    vsum[...] = total.reshape(EXPERTS, cap, WIN)
    own = pltpu.make_async_copy(vsum.at[e], rfin.at[e], load_sem.at[3])
    own.start()
    moves = []
    for d in range(1, EXPERTS):
        to = (e + d) % EXPERTS
        moves.append(send(vsum.at[to], rfin.at[e], at_dp(to * zl_n + zl, core)))
    own.wait()
    for cp in moves:
        cp.wait_recv()
    routed = nn(placed, rfin[...].reshape(EXPERTS * cap, WIN), lax.Precision.HIGHEST)
    turned = pltpu.roll(routed, feat, 1)
    out_ref[...] = jnp.where(odd == 1, turned, routed)[:, 0:feat]
    for cp in started:
        cp.wait_send()


def solution(mesh):
    zl_n = mesh.shape["dp"] // (EXPERTS * CORES)

    def local(tokens, upstream, route_ids, route_weights, w_gate, w_up, w_down):
        tok, feat = tokens.shape
        width, hid = w_gate.shape
        cap = tok // 2
        src_n = zl_n * EXPERTS
        rows, slots = src_n * tok // 2, src_n * cap // 2
        copies = 3 + 2 * (EXPERTS - 1) + 2 * (zl_n - 1) + 48
        vmem = pl.BlockSpec(memory_space=pltpu.VMEM)
        hbm = pl.BlockSpec(memory_space=pl.ANY)
        return pl.pallas_call(
            functools.partial(kernel, zl_n),
            out_shape=jax.ShapeDtypeStruct((tok, feat), F32),
            in_specs=[vmem] * 4 + [hbm] * 3,
            out_specs=vmem,
            scratch_shapes=[
                pltpu.VMEM((width, CORES * hid), BF16),
                pltpu.VMEM((width, CORES * hid), BF16),
                pltpu.VMEM((CORES * hid, width), BF16),
                pltpu.VMEM((EXPERTS, tok, WIN), BF16),
                pltpu.VMEM((2, RING, RING, rows, WIN), BF16),
                pltpu.VMEM((2 * rows, width), BF16),
                pltpu.VMEM((2 * slots, 2 * CORES * hid), BF16),
                pltpu.VMEM((2, RING, RING, slots, WIN), BF16),
                pltpu.VMEM((2, 2, RING, slots // 2, WIN), BF16),
                pltpu.VMEM((2, 2, RING, slots, WIN), BF16),
                pltpu.VMEM((2, RING, slots, WIN), F32),
                pltpu.VMEM((2, RING, slots, WIN), BF16),
                pltpu.VMEM((2, 2, slots // 2, WIN), BF16),
                pltpu.VMEM((2, 2, slots, WIN), BF16),
                pltpu.VMEM((zl_n, EXPERTS * cap, WIN), F32),
                pltpu.VMEM((zl_n, EXPERTS * cap, WIN), BF16),
                pltpu.VMEM((zl_n - 1, EXPERTS * cap, WIN), BF16),
                pltpu.VMEM((EXPERTS, cap, WIN), F32),
                pltpu.VMEM((EXPERTS, cap, WIN), F32),
                pltpu.SemaphoreType.DMA((4,)),
                pltpu.SemaphoreType.DMA((copies,)),
                pltpu.SemaphoreType.DMA((copies,)),
            ],
            compiler_params=pltpu.CompilerParams(
                collective_id=0, has_side_effects=True, vmem_limit_bytes=48 * 1024 * 1024
            ),
        )(tokens, upstream, route_ids, route_weights, w_gate, w_up, w_down)

    in_specs = (
        P("dp", "etp"),
        P("dp", "etp"),
        P("dp", None),
        P("dp", None),
        P(None, ("dp", "etp")),
        P(None, ("dp", "etp")),
        P(("dp", "etp"), None),
    )
    return jax.shard_map(local, mesh=mesh, in_specs=in_specs, out_specs=P("dp", "etp"), check_vma=False)
```

time: 475 us -> 118 us (0.25)
  waiting for transfers between devices: 217 us -> 0 us
  blocking collectives: 208 us -> 0 us
  Pallas kernels: 0 us -> 112 us
  matrix products: 21.5 us -> 0 us
  between operations: 13.2 us -> 0.02 us
  local copies, waits for them, and re-layouts: 12.1 us -> 4.89 us
    all_to_all x3 -> x0, blocking collectives: 208 us -> none  [the longest x1 89.1 us: local(): lax.all_to_all(returned, 'dp', split_axis=0, concat_axis=0, tiled=True)]
    unnamed x4 -> x0, waiting for transfers between devices: 117 us -> none
    pallas_call x0 -> x1, Pallas kernels: none -> 112 us  [local(): pl.pallas_call(functools.partial(kernel, zl_n), out_shape=jax.ShapeDtypeS...]
    all_gather x2 -> x0, waiting for transfers between devices: 99.7 us -> none  [the longest x1 84.3 us: local(): lax.all_gather(flat_x, 'etp', axis=1, tiled=True)]
    dot_general x7 -> x0, matrix products: 21.5 us -> none  [the longest x1 7.96 us: local(): lax.dot_general(w_gate, d_gate, (((1,), (1,)), ((), ())), preferred_eleme...]
  transfers between devices with their start and end apart: 3 -> 0, of which waited for: 3 -> 0; matrix products, arithmetic and copies ran while one was open for 1% -> 0% of each run, Pallas kernels for 0% -> 0%
where the time goes in v1:
time: 118 us; the launch traced here: 117 us
  Pallas kernels  112 us (95%)
  local copies, waits for them, and re-layouts  4.89 us (4%)
    pallas_call x1, Pallas kernels, local(): pl.pallas_call(functools.partial(kernel, zl_n), out_shape=jax.ShapeDtypeS...  112 us
    unnamed x15, local copies, waits for them, and re-layouts  4.89 us

profile of v1, /device:TPU:6, one launch (start us, length us, event | category | flops | bytes accessed | tf_op | source)
XLA Modules:
  0.0 117.0 jit_solution(5704692035252233008)
XLA Ops:
  0.0 0.0 copy-start.5
  0.0 0.0 copy-start.4
  0.0 0.0 copy-start.3
  0.0 0.8 copy.8.ids_ref
  0.8 0.0 copy-done.5
  0.8 0.1 copy.9.rw_ref
  0.9 0.0 copy-done.4
  0.9 0.0 copy-done.3
  0.9 0.0 copy-start
  0.9 1.1 copy-done
  2.0 0.0 copy-start.1
  2.0 1.1 copy-done.1
  3.2 0.0 copy-start.2
  3.2 1.1 copy-done.2
  4.3 112.1 %shard_map.73 = f32[16,192]{1,0:T(8,128)S(1)} custom-call(bf16[16,192]{1,0:T(8,128)(2,1)S(1)} %copy-done.3, bf16[16,192]{1,0:T(8,128)(2,1)S(1)} %copy-done.4, s32[16,2]{1,0:T(8,128)S(1)} %copy.8.ids_ref, f32[16,2]{1,0:T(8,128)S(1)} %copy.9.rw_ref, bf16[3072,128]{1,0:T(8,128)(2,1)S(1)} %copy-done, bf16[3072,128]{1,0:T(8,128)(2,1)S(1)} %copy-done.1, ...), custom_call_target="tpu_custom_call" | custom-call | tf_op jit(solution)/shard_map/pallas_call | solution.py:306
  116.4 0.6 copy.11
Async XLA Ops:
  0.0 0.8 copy-start.5
  0.0 0.9 copy-start.4
  0.0 0.9 copy-start.3
  0.9 1.1 copy-start
  2.0 1.1 copy-start.1
  3.2 1.1 copy-start.2

commit v2 on v1

v2 whole, which is shorter than its diff:
```python
import functools

import jax
import jax.numpy as jnp
from jax import lax
from jax.experimental import pallas as pl
from jax.experimental.pallas import tpu as pltpu
from jax.sharding import PartitionSpec as P

EXPERTS = 8
CORES = 2
RING = 4
ZL = 4
LANES = 128
F32 = jnp.float32
BF16 = jnp.bfloat16
MESH = pl.DeviceIdType.MESH


def nn(a, b, precision=None):
    return lax.dot_general(a, b, (((1,), (0,)), ((), ())), preferred_element_type=F32, precision=precision)


def nt(a, b, precision=None):
    return lax.dot_general(a, b, (((1,), (1,)), ((), ())), preferred_element_type=F32, precision=precision)


def tn(a, b):
    return lax.dot_general(a, b, (((0,), (0,)), ((), ())), preferred_element_type=F32)


def kernel(
    tok_hbm, up_hbm, ids_hbm, rw_hbm, wg_hbm, wu_hbm, wd_hbm,
    out_ref,
    tok_ref, up_ref, ids_ref, rw_ref, wg, wu, wd, blk, land, pbuf, zfull, dgu,
    ssum, sbuf, relay, main, tsum, thalf, relay2, main2, fsum, fhalf, zrecv, vsum, rfin,
    load_sem, send_sem, recv_sem,
):
    tok, feat = tok_ref.shape
    cap = tok // 2
    dp, etp = lax.axis_index("dp"), lax.axis_index("etp")
    core, z = dp % CORES, dp // CORES
    zl, e = z % ZL, z // ZL
    x, y = etp // RING, etp % RING
    odd, late = etp % 2, e // (EXPERTS // 2)
    counter = [0]
    started = []

    def at_dp(zz, cc):
        return {"dp": zz * CORES + cc}

    def at_xy(xx, yy):
        return {"etp": xx * RING + yy}

    def send(src, dst, device):
        k = counter[0]
        counter[0] += 1
        cp = pltpu.make_async_remote_copy(
            src_ref=src, dst_ref=dst, send_sem=send_sem.at[k], recv_sem=recv_sem.at[k], device_id=device,
            device_id_type=MESH,
        )
        cp.start()
        started.append(cp)
        return cp

    partners = [at_dp((e + d) % EXPERTS * ZL + zl, core) for d in range(1, EXPERTS)]
    partners += [at_dp(z, 1 - core)]
    partners += [at_dp(e * ZL + (zl + d) % ZL, core) for d in range(1, ZL)]
    partners += [at_xy((x + d) % RING, y) for d in (1, RING - 1)]
    partners += [at_xy(x, (y + d) % RING) for d in (1, RING - 1)]
    barrier = pltpu.get_barrier_semaphore()
    for device in partners:
        pl.semaphore_signal(barrier, inc=1, device_id=device, device_id_type=MESH)

    hid = wg_hbm.shape[1]
    loads = [
        pltpu.make_async_copy(src, dst, load_sem.at[k])
        for k, (src, dst) in enumerate([
            (ids_hbm, ids_ref), (rw_hbm, rw_ref), (tok_hbm, tok_ref), (up_hbm, up_ref),
            (wg_hbm, wg.at[:, 0:hid]), (wu_hbm, wu.at[:, 0:hid]), (wd_hbm, wd.at[0:hid, :]),
        ])
    ]
    for cp in loads:
        cp.start()
    for cp in loads[:4]:
        cp.wait()

    slot = lax.broadcasted_iota(jnp.int32, (EXPERTS * cap, tok), 0)
    slot_e, slot_s = slot >> 3, slot & 7
    ids = ids_ref[...]
    one0 = jnp.where(ids[0:1, :] == slot_e, 1.0, 0.0).astype(F32)
    one1 = jnp.where(ids[1:2, :] == slot_e, 1.0, 0.0).astype(F32)
    earlier = lax.broadcasted_iota(jnp.int32, (tok, tok), 0) < lax.broadcasted_iota(jnp.int32, (tok, tok), 1)
    before = nn(one0 + one1, jnp.where(earlier, 1.0, 0.0).astype(F32))
    fits = jnp.where(before == slot_s.astype(F32), 1.0, 0.0).astype(F32)
    p0, p1 = one0 * fits, one1 * fits
    placed = (p0 + p1).astype(BF16)
    f = lax.broadcasted_iota(jnp.int32, (feat, 2 * LANES), 0)
    rest = feat - LANES
    even_to = f + jnp.where(f >= LANES, late * rest, 0)
    odd_to = jnp.where(f >= rest, f - rest, LANES + f + (1 - late) * rest)
    to_lane = even_to + odd * (odd_to - even_to)
    spread = jnp.where(lax.broadcasted_iota(jnp.int32, (feat, 2 * LANES), 1) == to_lane, 1.0, 0.0).astype(F32)
    spread_half = spread.astype(BF16)
    xw = nn(tok_ref[...], spread_half).astype(BF16)
    uw = nn(up_ref[...], spread_half).astype(BF16)
    rw = rw_ref[...]
    scale = jnp.sum(p0 * rw[0:1, :] + p1 * rw[1:2, :], axis=1, keepdims=True)
    xs = nn(placed, xw).reshape(EXPERTS, cap, 2 * LANES)
    ds = (scale * nn(placed, uw)).reshape(EXPERTS, cap, 2 * LANES)
    blk[...] = jnp.concatenate([xs, ds], axis=1).astype(BF16)

    pl.semaphore_wait(barrier, len(partners))

    moves = []
    for d in (4, 3, 5, 2, 6, 1, 7):
        to = (e + d) % EXPERTS
        moves.append(send(blk.at[to], land.at[e], at_dp(to * ZL + zl, core)))
    land[e] = blk[e]
    sibling = at_dp(z, 1 - core)
    for cp in loads[4:]:
        cp.wait()
    weights = [
        send(wd_hbm, wd.at[hid:, :], sibling),
        send(wg_hbm, wg.at[:, hid:], sibling),
        send(wu_hbm, wu.at[:, hid:], sibling),
    ]
    for cp in moves:
        cp.wait_recv()
    half, zp = zl // 2, zl % 2
    pa, pb = x + half * (y - x), y + half * (x - y)
    group = EXPERTS * tok
    pair_src = EXPERTS // 2
    pbuf[half, pa, pb, zp, 0:group] = land[:, :, 0:LANES].reshape(group, LANES)
    pbuf[half, pa, pb, zp, group:] = (
        land[0:pair_src, :, LANES:] + land[pair_src:, :, LANES:]
    ).reshape(group // 2, LANES)
    region = pbuf.at[half, pa, pb, zp]
    moves = [send(region, region, at_dp(e * ZL + (zl + d) % ZL, core)) for d in (2, 1, 3)]
    for cp in moves:
        cp.wait_recv()

    def ahead(h, stage, step):
        if (h == 0) == (stage == 0):
            return at_xy((x + step) % RING, y)
        return at_xy(x, (y + step) % RING)

    def place(h):
        return (x, y) if h == 0 else (y, x)

    def unit(h, da, db, q=None):
        a, b = place(h)
        ref = pbuf.at[h, (a + da) % RING, (b + db) % RING]
        return ref if q is None else ref.at[q]

    def fan(h, stage, da, db, side, q=None):
        return send(unit(h, da, db, q), unit(h, da, db, q), ahead(h, stage, side))

    left, right = RING - 1, 1
    halves = range(2)
    s0 = [[fan(h, 0, 0, 0, right, 0), fan(h, 0, 0, 0, left, 1), fan(h, 0, 0, 0, right, 1), fan(h, 0, 0, 0, left, 0)] for h in halves]
    own = [[fan(h, 1, 0, 0, right), fan(h, 1, 0, 0, left)] for h in halves]
    over = [[], []]
    for h in halves:
        s0[h][0].wait_recv()
        over[h].append(fan(h, 0, left, 0, right, 0))
        s0[h][1].wait_recv()
        over[h].append(fan(h, 0, right, 0, left, 1))
    prev, following = [], []
    for h in halves:
        s0[h][2].wait_recv()
        prev.append([fan(h, 1, left, 0, right), fan(h, 1, left, 0, left)])
        s0[h][3].wait_recv()
        following.append([fan(h, 1, right, 0, right), fan(h, 1, right, 0, left)])
    tail = []
    opposite = []
    for h in halves:
        over[h][0].wait_recv()
        over[h][1].wait_recv()
        opposite.append([fan(h, 1, 2, 0, right, 0), fan(h, 1, 2, 0, left, 1), fan(h, 1, 2, 0, right, 1), fan(h, 1, 2, 0, left, 0)])
    for h in halves:
        own[h][0].wait_recv()
        tail.append(fan(h, 1, 0, left, right))
    for h in halves:
        prev[h][1].wait_recv()
        tail.append(fan(h, 1, left, right, left))
    for h in halves:
        following[h][0].wait_recv()
        tail.append(fan(h, 1, right, left, right, 0))
        following[h][1].wait_recv()
        tail.append(fan(h, 1, right, right, left, 1))
    for h in halves:
        opposite[h][0].wait_recv()
        tail.append(fan(h, 1, 2, left, right, 0))
        opposite[h][1].wait_recv()
        tail.append(fan(h, 1, 2, right, left, 1))
    for h in halves:
        for cp in (own[h][1], prev[h][0], opposite[h][2], opposite[h][3]):
            cp.wait_recv()
    for cp in tail:
        cp.wait_recv()
    for cp in weights:
        cp.wait_recv()

    pairs = RING * RING // 2
    wide = 2 * feat

    def pair_place(h, j):
        px, py = j // (RING // 2), j % (RING // 2) * 2
        return ((px, py), (px, py + 1)) if h == 0 else ((py, px), (py + 1, px))

    def low(shape):
        return lax.broadcasted_iota(jnp.int32, shape, 1) < rest

    for h in halves:
        for j in range(pairs):
            (a0, b0), (a1, b1) = pair_place(h, j)
            base = j * wide
            for q in range(2):
                row = (2 * h + q) * group
                mid = row + group // 2
                zfull[row:row + group, base:base + LANES] = pbuf[h, a0, b0, q, 0:group]
                zfull[row:row + group, base + 2 * LANES:base + wide] = pbuf[h, a1, b1, q, 0:group]
                even_mid = pbuf[h, a0, b0, q, group:].astype(F32)
                odd_mid = pbuf[h, a1, b1, q, group:].astype(F32)
                below = low(even_mid.shape)
                zfull[row:mid, base + LANES:base + 2 * LANES] = jnp.where(below, even_mid, odd_mid).astype(BF16)
                zfull[mid:row + group, base + LANES:base + 2 * LANES] = pltpu.roll(
                    jnp.where(below, odd_mid, even_mid), rest, 1
                ).astype(BF16)

    chip_hid = CORES * hid
    src = 2 * EXPERTS
    rows, slots = src * tok, src * cap
    for h in halves:
        act = zfull[h * rows:(h + 1) * rows, :]
        gate = nn(act, wg[...]).reshape(src, tok, chip_hid)[:, 0:cap].reshape(slots, chip_hid)
        up = nn(act, wu[...]).reshape(src, tok, chip_hid)[:, 0:cap].reshape(slots, chip_hid)
        back = nt(act, wd[...]).reshape(src, tok, chip_hid)[:, cap:tok].reshape(slots, chip_hid)
        sig = 1.0 / (1.0 + jnp.exp(-gate))
        dgu[h * slots:(h + 1) * slots, 0:chip_hid] = (back * up * sig * (1.0 + gate * (1.0 - sig))).astype(BF16)
        dgu[h * slots:(h + 1) * slots, chip_hid:] = (back * gate * sig).astype(BF16)
    per_zl = EXPERTS * cap

    def keep(h, a, b, q, r0, r1, value):
        ssum[h, a, b, q, r0:r1] = value
        sbuf[h, a, b, q, r0:r1] = value.astype(BF16)

    packed = per_zl * 3 // 2
    for j in range(pairs):
        part = nt(dgu[:, 0:chip_hid], wg[j * wide:(j + 1) * wide, :])
        part = part + nt(dgu[:, chip_hid:], wu[j * wide:(j + 1) * wide, :])
        for h in halves:
            (a0, b0), (a1, b1) = pair_place(h, j)
            for q in range(2):
                here = part[(2 * h + q) * per_zl:(2 * h + q + 1) * per_zl]
                keep(h, a0, b0, q, 0, per_zl, here[:, 0:LANES])
                keep(h, a1, b1, q, 0, per_zl, here[:, 2 * LANES:])
                first = here[0:per_zl // 2, LANES:2 * LANES]
                turned = pltpu.roll(here[per_zl // 2:, LANES:2 * LANES], rest, 1)
                below = low(first.shape)
                keep(h, a0, b0, q, per_zl, packed, jnp.where(below, first, turned))
                keep(h, a1, b1, q, per_zl, packed, jnp.where(below, turned, first))

    first = []
    for h in halves:
        a = place(h)[0]
        nxt, opp, prv = (a + 1) % RING, (a + 2) % RING, (a + 3) % RING
        first.append([
            send(sbuf.at[h, opp, :, 0], relay.at[h, 0], ahead(h, 0, right)),
            send(sbuf.at[h, opp, :, 1], relay.at[h, 1], ahead(h, 0, left)),
            send(sbuf.at[h, nxt, :, 1], main.at[h, 0, :, 1], ahead(h, 0, right)),
            send(sbuf.at[h, prv, :, 0], main.at[h, 1, :, 0], ahead(h, 0, left)),
        ])
    for h in halves:
        a = place(h)[0]
        nxt, prv = (a + 1) % RING, (a + 3) % RING
        first[h][0].wait_recv()
        sbuf[h, nxt, :, 0] = (ssum[h, nxt, :, 0] + relay[h, 0].astype(F32)).astype(BF16)
        first[h].append(send(sbuf.at[h, nxt, :, 0], main.at[h, 0, :, 0], ahead(h, 0, right)))
        first[h][1].wait_recv()
        sbuf[h, prv, :, 1] = (ssum[h, prv, :, 1] + relay[h, 1].astype(F32)).astype(BF16)
        first[h].append(send(sbuf.at[h, prv, :, 1], main.at[h, 1, :, 1], ahead(h, 0, left)))
    second = []
    for h in halves:
        for cp in first[h][2:]:
            cp.wait_recv()
        a, b = place(h)
        total = ssum[h, a] + main[h, 0].astype(F32) + main[h, 1].astype(F32)
        tsum[h] = total
        thalf[h] = total.astype(BF16)
        nxt, opp, prv = (b + 1) % RING, (b + 2) % RING, (b + 3) % RING
        second.append([
            send(thalf.at[h, opp, 0], relay2.at[h, 0], ahead(h, 1, right)),
            send(thalf.at[h, opp, 1], relay2.at[h, 1], ahead(h, 1, left)),
            send(thalf.at[h, nxt, 1], main2.at[h, 0, 1], ahead(h, 1, right)),
            send(thalf.at[h, prv, 0], main2.at[h, 1, 0], ahead(h, 1, left)),
        ])
    for h in halves:
        b = place(h)[1]
        nxt, prv = (b + 1) % RING, (b + 3) % RING
        second[h][0].wait_recv()
        thalf[h, nxt, 0] = (tsum[h, nxt, 0] + relay2[h, 0].astype(F32)).astype(BF16)
        second[h].append(send(thalf.at[h, nxt, 0], main2.at[h, 0, 0], ahead(h, 1, right)))
        second[h][1].wait_recv()
        thalf[h, prv, 1] = (tsum[h, prv, 1] + relay2[h, 1].astype(F32)).astype(BF16)
        second[h].append(send(thalf.at[h, prv, 1], main2.at[h, 1, 1], ahead(h, 1, left)))
    for h in halves:
        for cp in second[h][2:]:
            cp.wait_recv()
        b = place(h)[1]
        total = tsum[h, b] + main2[h, 0].astype(F32) + main2[h, 1].astype(F32)
        fsum[2 * h:2 * h + 2] = total
        fhalf[2 * h:2 * h + 2] = total.astype(BF16)

    moves = []
    for d in (2, 1, 3):
        to = (zl + d) % ZL
        moves.append(send(fhalf.at[to], zrecv.at[d - 1], at_dp(e * ZL + to, core)))
    for cp in moves:
        cp.wait_recv()
    total = fsum[zl]
    for d in range(1, ZL):
        total = total + zrecv[d - 1].astype(F32)
    mids = total[per_zl:].reshape(EXPERTS // 2, cap, LANES)
    mids = jnp.concatenate([mids, mids], axis=0)
    vsum[...] = jnp.concatenate([total[0:per_zl].reshape(EXPERTS, cap, LANES), mids], axis=1).astype(BF16)
    moves = []
    for d in (4, 3, 5, 2, 6, 1, 7):
        to = (e + d) % EXPERTS
        moves.append(send(vsum.at[to], rfin.at[e], at_dp(to * ZL + zl, core)))
    rfin[e] = vsum[e]
    for cp in moves:
        cp.wait_recv()
    got = rfin[...].astype(F32)
    got = jnp.concatenate(
        [got[:, 0:cap].reshape(EXPERTS * cap, LANES), got[:, cap:].reshape(EXPERTS * cap, LANES)], axis=1
    )
    out_ref[...] = nt(tn(placed, got.astype(BF16)), spread, lax.Precision.HIGHEST)
    for cp in started:
        cp.wait_send()


def solution(mesh):
    def local(tokens, upstream, route_ids, route_weights, w_gate, w_up, w_down):
        tok, feat = tokens.shape
        width, hid = w_gate.shape
        cap = tok // 2
        group, per_zl = EXPERTS * tok, EXPERTS * cap
        unit, packed = group * 3 // 2, per_zl * 3 // 2
        copies = 3 + 2 * (EXPERTS - 1) + 2 * (ZL - 1) + 44 + 24
        hbm = pl.BlockSpec(memory_space=pltpu.HBM)
        return pl.pallas_call(
            kernel,
            out_shape=jax.ShapeDtypeStruct((tok, feat), F32),
            in_specs=[hbm] * 7,
            out_specs=pl.BlockSpec(memory_space=pltpu.VMEM),
            scratch_shapes=[
                pltpu.VMEM((tok, feat), BF16),
                pltpu.VMEM((tok, feat), BF16),
                pltpu.VMEM((2, tok), jnp.int32),
                pltpu.VMEM((2, tok), F32),
                pltpu.VMEM((width, CORES * hid), BF16),
                pltpu.VMEM((width, CORES * hid), BF16),
                pltpu.VMEM((CORES * hid, width), BF16),
                pltpu.VMEM((EXPERTS, tok, 2 * LANES), BF16),
                pltpu.VMEM((EXPERTS, tok, 2 * LANES), BF16),
                pltpu.VMEM((2, RING, RING, 2, unit, LANES), BF16),
                pltpu.VMEM((ZL * group, width), BF16),
                pltpu.VMEM((ZL * per_zl, 2 * CORES * hid), BF16),
                pltpu.VMEM((2, RING, RING, 2, packed, LANES), F32),
                pltpu.VMEM((2, RING, RING, 2, packed, LANES), BF16),
                pltpu.VMEM((2, 2, RING, packed, LANES), BF16),
                pltpu.VMEM((2, 2, RING, 2, packed, LANES), BF16),
                pltpu.VMEM((2, RING, 2, packed, LANES), F32),
                pltpu.VMEM((2, RING, 2, packed, LANES), BF16),
                pltpu.VMEM((2, 2, packed, LANES), BF16),
                pltpu.VMEM((2, 2, 2, packed, LANES), BF16),
                pltpu.VMEM((ZL, packed, LANES), F32),
                pltpu.VMEM((ZL, packed, LANES), BF16),
                pltpu.VMEM((ZL - 1, packed, LANES), BF16),
                pltpu.VMEM((EXPERTS, tok, LANES), BF16),
                pltpu.VMEM((EXPERTS, tok, LANES), BF16),
                pltpu.SemaphoreType.DMA((7,)),
                pltpu.SemaphoreType.DMA((copies,)),
                pltpu.SemaphoreType.DMA((copies,)),
            ],
            compiler_params=pltpu.CompilerParams(
                collective_id=0, has_side_effects=True, vmem_limit_bytes=63 * 1024 * 1024
            ),
        )(tokens, upstream, route_ids.T, route_weights.T, w_gate, w_up, w_down)

    in_specs = (
        P("dp", "etp"),
        P("dp", "etp"),
        P("dp", None),
        P("dp", None),
        P(None, ("dp", "etp")),
        P(None, ("dp", "etp")),
        P(("dp", "etp"), None),
    )
    return jax.shard_map(local, mesh=mesh, in_specs=in_specs, out_specs=P("dp", "etp"), check_vma=False)
```

time: 118 us -> 104 us (0.88)
  Pallas kernels: 112 us -> 103 us
  local copies, waits for them, and re-layouts: 4.89 us -> 1.32 us
    pallas_call x1, Pallas kernels: 112 us -> 103 us  [local(): pl.pallas_call(kernel, out_shape=jax.ShapeDtypeStruct((tok, feat), F32),...]
    unnamed x15 -> x1, local copies, waits for them, and re-layouts: 4.89 us -> 1.32 us
where the time goes in v2:
time: 104 us
  Pallas kernels  103 us (99%)
  local copies, waits for them, and re-layouts  1.32 us (1%)
    pallas_call x1, Pallas kernels, local(): pl.pallas_call(kernel, out_shape=jax.ShapeDtypeStruct((tok, feat), F32),...  103 us

profile of v2, /device:TPU:6, one launch (start us, length us, event | category | flops | bytes accessed | tf_op | source)
XLA Modules:
  0.0 104.2 jit_solution(501027601238737203)
XLA Ops:
  0.0 102.8 %shard_map.73 = f32[16,192]{1,0:T(8,128)} custom-call(bf16[16,192]{1,0:T(8,128)(2,1)} %tok_hbm.1, bf16[16,192]{1,0:T(8,128)(2,1)} %up_hbm.1, s32[2,16]{1,0:T(2,128)} %bitcast.2, f32[2,16]{1,0:T(2,128)} %bitcast.3, bf16[3072,128]{1,0:T(8,128)(2,1)} %wg_hbm.1, bf16[3072,128]{1,0:T(8,128)(2,1)} %wu_hbm.1, bf16[128,3072]{1,0:T(8,128)(2,1)} %wd_hbm.1), custom_call_target="tpu_custom_call" | custom-call | tf_op jit(solution)/shard_map/pallas_call | solution.py:353
  102.8 1.3 %copy.9 = f32[16,192]{1,0:T(8,128)} copy(f32[16,192]{1,0:T(8,128)} %shard_map.73) | data formatting | bytes 24576

commit v3 on v0

v3 whole, which is shorter than its diff:
```python
import functools

import jax
import jax.numpy as jnp
from jax import lax
from jax.experimental import pallas as pl
from jax.experimental.pallas import tpu as pltpu
from jax.sharding import PartitionSpec as P

EXPERTS = 8
CORES = 2
RING = 4
ZL = 4
LANES = 128
BATCHES = ((0, 1, 7, 2), (6, 3, 5, 4))
MID_HALF = [next(k // 2 for batch in BATCHES for k, b in enumerate(batch) if b == d) for d in range(EXPERTS)]
ORDER = "nnnfnfnnffnwnffnffnfnfnfnff"
F32 = jnp.float32
BF16 = jnp.bfloat16
MESH = pl.DeviceIdType.MESH


def nn(a, b, precision=None):
    return lax.dot_general(a, b, (((1,), (0,)), ((), ())), preferred_element_type=F32, precision=precision)


def nt(a, b, precision=None):
    return lax.dot_general(a, b, (((1,), (1,)), ((), ())), preferred_element_type=F32, precision=precision)


def tn(a, b):
    return lax.dot_general(a, b, (((0,), (0,)), ((), ())), preferred_element_type=F32)


def kernel(
    tok_hbm, up_hbm, ids_hbm, rw_hbm, wg_hbm, wu_hbm, wd_hbm,
    out_ref,
    tok_ref, up_ref, ids_ref, rw_ref, wg, wu, wd, blk, land, pbuf, zfull, dgu,
    ssum, sbuf, relay, main, tsum, thalf, main2, fsum, fhalf, zrecv, vsum, rfin,
    load_sem, send_sem, recv_sem,
):
    tok, feat = tok_ref.shape
    cap = tok // 2
    dp, etp = lax.axis_index("dp"), lax.axis_index("etp")
    core, z = dp % CORES, dp // CORES
    zl, e = z % ZL, z // ZL
    x, y = etp // RING, etp % RING
    odd = etp % 2
    counter = [0]
    started = []

    def at_dp(zz, cc):
        return {"dp": zz * CORES + cc}

    def at_xy(xx, yy):
        return {"etp": xx * RING + yy}

    def send(src, dst, device):
        k = counter[0]
        counter[0] += 1
        cp = pltpu.make_async_remote_copy(
            src_ref=src, dst_ref=dst, send_sem=send_sem.at[k], recv_sem=recv_sem.at[k], device_id=device,
            device_id_type=MESH,
        )
        cp.start()
        started.append(cp)
        return cp

    partners = [at_dp((e + d) % EXPERTS * ZL + zl, core) for d in range(1, EXPERTS)]
    partners += [at_dp(z, 1 - core)]
    partners += [at_dp(e * ZL + (zl + d) % ZL, core) for d in range(1, ZL)]
    partners += [at_xy((x + d) % RING, y) for d in range(1, RING)]
    partners += [at_xy(x, (y + d) % RING) for d in range(1, RING)]
    barrier = pltpu.get_barrier_semaphore()
    for device in partners:
        pl.semaphore_signal(barrier, inc=1, device_id=device, device_id_type=MESH)

    hid = wg_hbm.shape[1]
    loads = [
        pltpu.make_async_copy(src, dst, load_sem.at[k])
        for k, (src, dst) in enumerate([
            (ids_hbm, ids_ref), (rw_hbm, rw_ref), (tok_hbm, tok_ref), (up_hbm, up_ref),
            (wg_hbm, wg.at[:, 0:hid]), (wu_hbm, wu.at[:, 0:hid]), (wd_hbm, wd.at[0:hid, :]),
        ])
    ]
    for cp in loads:
        cp.start()
    for cp in loads[:4]:
        cp.wait()

    slot = lax.broadcasted_iota(jnp.int32, (EXPERTS * cap, tok), 0)
    slot_e, slot_s = (e - (slot >> 3) + EXPERTS) & (EXPERTS - 1), slot & 7
    ids = ids_ref[...]
    one0 = jnp.where(ids[0:1, :] == slot_e, 1.0, 0.0).astype(F32)
    one1 = jnp.where(ids[1:2, :] == slot_e, 1.0, 0.0).astype(F32)
    earlier = lax.broadcasted_iota(jnp.int32, (tok, tok), 0) < lax.broadcasted_iota(jnp.int32, (tok, tok), 1)
    before = nn(one0 + one1, jnp.where(earlier, 1.0, 0.0).astype(F32))
    fits = jnp.where(before == slot_s.astype(F32), 1.0, 0.0).astype(F32)
    p0, p1 = one0 * fits, one1 * fits
    placed = (p0 + p1).astype(BF16)
    rest = feat - LANES
    f = lax.broadcasted_iota(jnp.int32, (feat, 3 * LANES), 0)
    lane = lax.broadcasted_iota(jnp.int32, (feat, 3 * LANES), 1)
    odd_to = jnp.where(f >= rest, f - rest, feat + f)
    to0 = f + odd * (odd_to - f)
    even_also = jnp.where(f >= LANES, feat + f, -1)
    odd_also = jnp.where(f >= rest, -1, feat + rest + f)
    to1 = even_also + odd * (odd_also - even_also)
    spread = jnp.where(lane == to0, 1.0, 0.0).astype(F32) + jnp.where(lane == to1, 1.0, 0.0).astype(F32)
    spread_half = spread.astype(BF16)
    xw = nn(tok_ref[...], spread_half).astype(BF16)
    uw = nn(up_ref[...], spread_half).astype(BF16)
    rw = rw_ref[...]
    scale = jnp.sum(p0 * rw[0:1, :] + p1 * rw[1:2, :], axis=1, keepdims=True)
    xs = nn(placed, xw).reshape(EXPERTS, cap, 3 * LANES)
    ds = (scale * nn(placed, uw)).reshape(EXPERTS, cap, 3 * LANES)
    both = jnp.concatenate([xs, ds], axis=1).astype(BF16)
    for d in range(EXPERTS):
        blk[d, :, 0:LANES] = both[d, :, 0:LANES]
        m = LANES * (1 + MID_HALF[d])
        blk[d, :, LANES:] = both[d, :, m:m + LANES]

    pl.semaphore_wait(barrier, len(partners))

    arrive = {}
    for d in (4, 5, 3, 6, 2, 7, 1):
        arrive[d] = send(blk.at[d], land.at[d], at_dp((e - d + EXPERTS) % EXPERTS * ZL + zl, core))
    land[0] = blk[0]
    sibling = at_dp(z, 1 - core)
    for cp in loads[4:]:
        cp.wait()
    weights = [
        send(wd_hbm, wd.at[hid:, :], sibling),
        send(wg_hbm, wg.at[:, hid:], sibling),
        send(wu_hbm, wu.at[:, hid:], sibling),
    ]
    half, zp = zl // 2, zl % 2
    pa, pb = x + half * (y - x), y + half * (x - y)
    per = len(BATCHES[0])
    group, chip_hid = per * tok, CORES * hid
    left, right = RING - 1, 1
    halves = range(2)
    pairs = RING * RING // 2
    wide = 2 * feat
    src = ZL * per
    rows, slots = src * tok, src * cap
    per_zl = per * cap
    packed = per_zl * 3 // 2

    def ahead(h, stage, step):
        if (h == 0) == (stage == 0):
            return at_xy((x + step) % RING, y)
        return at_xy(x, (y + step) % RING)

    def place(h):
        return (x, y) if h == 0 else (y, x)

    def pair_place(h, j):
        px, py = j // (RING // 2), j % (RING // 2) * 2
        return ((px, py), (px, py + 1)) if h == 0 else ((py, px), (py + 1, px))

    def low(shape):
        return lax.broadcasted_iota(jnp.int32, shape, 1) < rest

    def work(n):
        batch = BATCHES[n]

        def fan(h, stage, da, db, side, q=None):
            a, b = place(h)
            ref = pbuf.at[n, h, (a + da) % RING, (b + db) % RING]
            ref = ref if q is None else ref.at[q]
            return send(ref, ref, ahead(h, stage, side))

        for d in batch:
            if d:
                arrive[d].wait_recv()
        for k, d in enumerate(batch):
            pbuf[n, half, pa, pb, zp, k * tok:(k + 1) * tok] = land[d, :, 0:LANES]
        for k in range(per // 2):
            pbuf[n, half, pa, pb, zp, group + k * tok:group + (k + 1) * tok] = (
                land[batch[k], :, LANES:] + land[batch[k + per // 2], :, LANES:]
            )
        region = pbuf.at[n, half, pa, pb, zp]
        moves = [send(region, region, at_dp(e * ZL + (zl + d) % ZL, core)) for d in (2, 1, 3)]
        yield "z"
        for cp in moves:
            cp.wait_recv()
        s0 = [[fan(h, 0, 0, 0, side) for side in (right, left, 2)] for h in halves]
        own = [[fan(h, 1, 0, 0, right), fan(h, 1, 0, 0, left)] for h in halves]
        yield "own"
        prev, following = [], []
        for h in halves:
            s0[h][0].wait_recv()
            prev.append([fan(h, 1, left, 0, right), fan(h, 1, left, 0, left)])
            s0[h][1].wait_recv()
            following.append([fan(h, 1, right, 0, right), fan(h, 1, right, 0, left)])
        yield "side"
        tail, opposite = [], []
        for h in halves:
            s0[h][2].wait_recv()
            opposite.append([fan(h, 1, 2, 0, right, 0), fan(h, 1, 2, 0, left, 1), fan(h, 1, 2, 0, right, 1), fan(h, 1, 2, 0, left, 0)])
        yield "opposite"
        for h in halves:
            own[h][0].wait_recv()
            tail.append(fan(h, 1, 0, left, right))
        for h in halves:
            prev[h][1].wait_recv()
            tail.append(fan(h, 1, left, right, left))
        yield "tail"
        for h in halves:
            following[h][0].wait_recv()
            tail.append(fan(h, 1, right, left, right, 0))
            following[h][1].wait_recv()
            tail.append(fan(h, 1, right, right, left, 1))
        for h in halves:
            opposite[h][0].wait_recv()
            tail.append(fan(h, 1, 2, left, right, 0))
            opposite[h][1].wait_recv()
            tail.append(fan(h, 1, 2, right, left, 1))
        yield "tail"
        for h in halves:
            for cp in (own[h][1], prev[h][0], opposite[h][2], opposite[h][3]):
                cp.wait_recv()
        for cp in tail:
            cp.wait_recv()
        for h in halves:
            for j in range(pairs):
                (a0, b0), (a1, b1) = pair_place(h, j)
                base = j * wide
                for q in range(2):
                    row = (2 * h + q) * group
                    mid = row + group // 2
                    zfull[n, row:row + group, base:base + LANES] = pbuf[n, h, a0, b0, q, 0:group]
                    zfull[n, row:row + group, base + 2 * LANES:base + wide] = pbuf[n, h, a1, b1, q, 0:group]
                    even_mid = pbuf[n, h, a0, b0, q, group:].astype(F32)
                    odd_mid = pbuf[n, h, a1, b1, q, group:].astype(F32)
                    below = low(even_mid.shape)
                    zfull[n, row:mid, base + LANES:base + 2 * LANES] = jnp.where(below, even_mid, odd_mid).astype(BF16)
                    zfull[n, mid:row + group, base + LANES:base + 2 * LANES] = pltpu.roll(
                        jnp.where(below, odd_mid, even_mid), rest, 1
                    ).astype(BF16)
        yield "merged"
        act = zfull[n]
        gate = nn(act, wg[...]).reshape(src, tok, chip_hid)[:, 0:cap].reshape(slots, chip_hid)
        up = nn(act, wu[...]).reshape(src, tok, chip_hid)[:, 0:cap].reshape(slots, chip_hid)
        back = nt(act, wd[...]).reshape(src, tok, chip_hid)[:, cap:tok].reshape(slots, chip_hid)
        sig = 1.0 / (1.0 + jnp.exp(-gate))
        dgu[n, :, 0:chip_hid] = (back * up * sig * (1.0 + gate * (1.0 - sig))).astype(BF16)
        dgu[n, :, chip_hid:] = (back * gate * sig).astype(BF16)
        yield "forward"

        def keep(h, a, b, q, r0, r1, value):
            ssum[n, h, a, b, q, r0:r1] = value
            sbuf[n, h, a, b, q, r0:r1] = value.astype(BF16)

        for j in range(pairs):
            part = nt(dgu[n, :, 0:chip_hid], wg[j * wide:(j + 1) * wide, :])
            part = part + nt(dgu[n, :, chip_hid:], wu[j * wide:(j + 1) * wide, :])
            for h in halves:
                (a0, b0), (a1, b1) = pair_place(h, j)
                for q in range(2):
                    here = part[(2 * h + q) * per_zl:(2 * h + q + 1) * per_zl]
                    keep(h, a0, b0, q, 0, per_zl, here[:, 0:LANES])
                    keep(h, a1, b1, q, 0, per_zl, here[:, 2 * LANES:])
                    lo = here[0:per_zl // 2, LANES:2 * LANES]
                    turned = pltpu.roll(here[per_zl // 2:, LANES:2 * LANES], rest, 1)
                    below = low(lo.shape)
                    keep(h, a0, b0, q, per_zl, packed, jnp.where(below, lo, turned))
                    keep(h, a1, b1, q, per_zl, packed, jnp.where(below, turned, lo))
        first = []
        for h in halves:
            a = place(h)[0]
            nxt, opp, prv = (a + 1) % RING, (a + 2) % RING, (a + 3) % RING
            first.append([
                send(sbuf.at[n, h, opp, :, 0], relay.at[n, h, 0], ahead(h, 0, right)),
                send(sbuf.at[n, h, opp, :, 1], relay.at[n, h, 1], ahead(h, 0, left)),
                send(sbuf.at[n, h, nxt, :, 1], main.at[n, h, 0, :, 1], ahead(h, 0, right)),
                send(sbuf.at[n, h, prv, :, 0], main.at[n, h, 1, :, 0], ahead(h, 0, left)),
            ])
        yield "backward"
        for h in halves:
            a = place(h)[0]
            nxt, prv = (a + 1) % RING, (a + 3) % RING
            first[h][0].wait_recv()
            sbuf[n, h, nxt, :, 0] = (ssum[n, h, nxt, :, 0] + relay[n, h, 0].astype(F32)).astype(BF16)
            first[h].append(send(sbuf.at[n, h, nxt, :, 0], main.at[n, h, 0, :, 0], ahead(h, 0, right)))
            first[h][1].wait_recv()
            sbuf[n, h, prv, :, 1] = (ssum[n, h, prv, :, 1] + relay[n, h, 1].astype(F32)).astype(BF16)
            first[h].append(send(sbuf.at[n, h, prv, :, 1], main.at[n, h, 1, :, 1], ahead(h, 0, left)))
        yield "relayed"
        second = []
        for h in halves:
            for cp in first[h][2:]:
                cp.wait_recv()
            a, b = place(h)
            total = ssum[n, h, a] + main[n, h, 0].astype(F32) + main[n, h, 1].astype(F32)
            tsum[n, h] = total
            thalf[n, h] = total.astype(BF16)
            second.append([
                send(thalf.at[n, h, (b + d) % RING], main2.at[n, h, d - 1], ahead(h, 1, d)) for d in (2, 1, 3)
            ])
        yield "summed"
        for h in halves:
            for cp in second[h]:
                cp.wait_recv()
            total = tsum[n, h, place(h)[1]]
            for d in range(1, RING):
                total = total + main2[n, h, d - 1].astype(F32)
            fsum[n, 2 * h:2 * h + 2] = total
            fhalf[n, 2 * h:2 * h + 2] = total.astype(BF16)
        moves = []
        for d in (2, 1, 3):
            to = (zl + d) % ZL
            moves.append(send(fhalf.at[n, to], zrecv.at[n, d - 1], at_dp(e * ZL + to, core)))
        yield "summed"
        for cp in moves:
            cp.wait_recv()
        total = fsum[n, zl]
        for d in range(1, ZL):
            total = total + zrecv[n, d - 1].astype(F32)
        mids = total[per_zl:].reshape(per // 2, cap, LANES)
        mids = jnp.concatenate([mids, mids], axis=0)
        vsum[n] = jnp.concatenate([total[0:per_zl].reshape(per, cap, LANES), mids], axis=1).astype(BF16)
        for k, d in reversed(list(enumerate(batch))):
            if d:
                returned.append(send(vsum.at[n, k], rfin.at[d], at_dp((e + d) % EXPERTS * ZL + zl, core)))
            else:
                rfin[0] = vsum[n, k]
        yield "back"

    returned = []
    near, far = work(0), work(1)
    for step in ORDER:
        if step == "w":
            for cp in weights:
                cp.wait_recv()
        else:
            next(near if step == "n" else far)
    for cp in returned:
        cp.wait_recv()
    got = rfin[...].astype(F32)
    mains, mids = got[:, 0:cap].reshape(EXPERTS * cap, LANES), got[:, cap:]
    empty = jnp.zeros((cap, LANES), F32)
    mids0 = jnp.concatenate([empty if MID_HALF[d] else mids[d] for d in range(EXPERTS)], axis=0)
    mids1 = jnp.concatenate([mids[d] if MID_HALF[d] else empty for d in range(EXPERTS)], axis=0)
    got = jnp.concatenate([mains, mids0, mids1], axis=1).astype(BF16)
    out_ref[...] = nt(tn(placed, got), spread, lax.Precision.HIGHEST)
    for cp in started:
        cp.wait_send()


def solution(mesh):
    def local(tokens, upstream, route_ids, route_weights, w_gate, w_up, w_down):
        tok, feat = tokens.shape
        width, hid = w_gate.shape
        cap = tok // 2
        per = EXPERTS // 2
        group, per_zl = per * tok, per * cap
        unit, packed = group * 3 // 2, per_zl * 3 // 2
        copies = 3 + 2 * (EXPERTS - 1) + 2 * (2 * (ZL - 1) + 38 + 18)
        hbm = pl.BlockSpec(memory_space=pltpu.HBM)
        return pl.pallas_call(
            kernel,
            out_shape=jax.ShapeDtypeStruct((tok, feat), F32),
            in_specs=[hbm] * 7,
            out_specs=pl.BlockSpec(memory_space=pltpu.VMEM),
            scratch_shapes=[
                pltpu.VMEM((tok, feat), BF16),
                pltpu.VMEM((tok, feat), BF16),
                pltpu.VMEM((2, tok), jnp.int32),
                pltpu.VMEM((2, tok), F32),
                pltpu.VMEM((width, CORES * hid), BF16),
                pltpu.VMEM((width, CORES * hid), BF16),
                pltpu.VMEM((CORES * hid, width), BF16),
                pltpu.VMEM((EXPERTS, tok, 2 * LANES), BF16),
                pltpu.VMEM((EXPERTS, tok, 2 * LANES), BF16),
                pltpu.VMEM((2, 2, RING, RING, 2, unit, LANES), BF16),
                pltpu.VMEM((2, ZL * group, width), BF16),
                pltpu.VMEM((2, ZL * per_zl, 2 * CORES * hid), BF16),
                pltpu.VMEM((2, 2, RING, RING, 2, packed, LANES), F32),
                pltpu.VMEM((2, 2, RING, RING, 2, packed, LANES), BF16),
                pltpu.VMEM((2, 2, 2, RING, packed, LANES), BF16),
                pltpu.VMEM((2, 2, 2, RING, 2, packed, LANES), BF16),
                pltpu.VMEM((2, 2, RING, 2, packed, LANES), F32),
                pltpu.VMEM((2, 2, RING, 2, packed, LANES), BF16),
                pltpu.VMEM((2, 2, RING - 1, 2, packed, LANES), BF16),
                pltpu.VMEM((2, ZL, packed, LANES), F32),
                pltpu.VMEM((2, ZL, packed, LANES), BF16),
                pltpu.VMEM((2, ZL - 1, packed, LANES), BF16),
                pltpu.VMEM((2, per, tok, LANES), BF16),
                pltpu.VMEM((EXPERTS, tok, LANES), BF16),
                pltpu.SemaphoreType.DMA((7,)),
                pltpu.SemaphoreType.DMA((copies,)),
                pltpu.SemaphoreType.DMA((copies,)),
            ],
            compiler_params=pltpu.CompilerParams(
                collective_id=0, has_side_effects=True, vmem_limit_bytes=63 * 1024 * 1024
            ),
        )(tokens, upstream, route_ids.T, route_weights.T, w_gate, w_up, w_down)

    in_specs = (
        P("dp", "etp"),
        P("dp", "etp"),
        P("dp", None),
        P("dp", None),
        P(None, ("dp", "etp")),
        P(None, ("dp", "etp")),
        P(("dp", "etp"), None),
    )
    return jax.shard_map(local, mesh=mesh, in_specs=in_specs, out_specs=P("dp", "etp"), check_vma=False)
```

time: 475 us -> 96.7 us (0.20)
  waiting for transfers between devices: 217 us -> 0 us
  blocking collectives: 208 us -> 0 us
  Pallas kernels: 0 us -> 94.7 us
  matrix products: 21.5 us -> 0 us
  between operations: 13.2 us -> 0.01 us
  local copies, waits for them, and re-layouts: 12.1 us -> 1.32 us
    all_to_all x3 -> x0, blocking collectives: 208 us -> none  [the longest x1 89.1 us: local(): lax.all_to_all(returned, 'dp', split_axis=0, concat_axis=0, tiled=True)]
    unnamed x4 -> x0, waiting for transfers between devices: 117 us -> none
    all_gather x2 -> x0, waiting for transfers between devices: 99.7 us -> none  [the longest x1 84.3 us: local(): lax.all_gather(flat_x, 'etp', axis=1, tiled=True)]
    pallas_call x0 -> x1, Pallas kernels: none -> 94.7 us  [local(): pl.pallas_call(kernel, out_shape=jax.ShapeDtypeStruct((tok, feat), F32),...]
    dot_general x7 -> x0, matrix products: 21.5 us -> none  [the longest x1 7.96 us: local(): lax.dot_general(w_gate, d_gate, (((1,), (1,)), ((), ())), preferred_eleme...]
    unnamed x9 -> x1, local copies, waits for them, and re-layouts: 8.56 us -> 1.32 us
  transfers between devices with their start and end apart: 3 -> 0, of which waited for: 3 -> 0; matrix products, arithmetic and copies ran while one was open for 1% -> 0% of each run, Pallas kernels for 0% -> 0%
where the time goes in v3:
time: 96.7 us; the launch traced here: 96 us
  Pallas kernels  94.7 us (98%)
  local copies, waits for them, and re-layouts  1.32 us (1%)
    pallas_call x1, Pallas kernels, local(): pl.pallas_call(kernel, out_shape=jax.ShapeDtypeStruct((tok, feat), F32),...  94.7 us

profile of v3, /device:TPU:6, one launch (start us, length us, event | category | flops | bytes accessed | tf_op | source)
XLA Modules:
  0.0 96.0 jit_solution(9249141726066132360)
XLA Ops:
  0.0 94.7 %shard_map.73 = f32[16,192]{1,0:T(8,128)} custom-call(bf16[16,192]{1,0:T(8,128)(2,1)} %tok_hbm.1, bf16[16,192]{1,0:T(8,128)(2,1)} %up_hbm.1, s32[2,16]{1,0:T(2,128)} %bitcast.2, f32[2,16]{1,0:T(2,128)} %bitcast.3, bf16[3072,128]{1,0:T(8,128)(2,1)} %wg_hbm.1, bf16[3072,128]{1,0:T(8,128)(2,1)} %wu_hbm.1, bf16[128,3072]{1,0:T(8,128)(2,1)} %wd_hbm.1), custom_call_target="tpu_custom_call" | custom-call | tf_op jit(solution)/shard_map/pallas_call | solution.py:362
  94.7 1.3 %copy.9 = f32[16,192]{1,0:T(8,128)} copy(f32[16,192]{1,0:T(8,128)} %shard_map.73) | data formatting | bytes 24576

commit v4 on v3

--- a/solution.py
+++ b/solution.py
@@ -14,6 +14,7 @@
 LANES = 128
 BATCHES = ((0, 1, 7, 2), (6, 3, 5, 4))
 MID_HALF = [next(k // 2 for batch in BATCHES for k, b in enumerate(batch) if b == d) for d in range(EXPERTS)]
+STRAIGHT = (1,)
 ORDER = "nnnfnfnnffnwnffnffnfnfnfnff"
 F32 = jnp.float32
 BF16 = jnp.bfloat16
@@ -270,15 +271,22 @@
         first = []
         for h in halves:
             a = place(h)[0]
+            if n in STRAIGHT:
+                first.append([
+                    send(sbuf.at[n, h, (a + d) % RING], main.at[n, h, d - 1], ahead(h, 0, d)) for d in (2, 1, 3)
+                ])
+                continue
             nxt, opp, prv = (a + 1) % RING, (a + 2) % RING, (a + 3) % RING
             first.append([
                 send(sbuf.at[n, h, opp, :, 0], relay.at[n, h, 0], ahead(h, 0, right)),
                 send(sbuf.at[n, h, opp, :, 1], relay.at[n, h, 1], ahead(h, 0, left)),
                 send(sbuf.at[n, h, nxt, :, 1], main.at[n, h, 0, :, 1], ahead(h, 0, right)),
-                send(sbuf.at[n, h, prv, :, 0], main.at[n, h, 1, :, 0], ahead(h, 0, left)),
+                send(sbuf.at[n, h, prv, :, 0], main.at[n, h, 2, :, 0], ahead(h, 0, left)),
             ])
         yield "backward"
         for h in halves:
+            if n in STRAIGHT:
+                continue
             a = place(h)[0]
             nxt, prv = (a + 1) % RING, (a + 3) % RING
             first[h][0].wait_recv()
@@ -286,14 +294,16 @@
             first[h].append(send(sbuf.at[n, h, nxt, :, 0], main.at[n, h, 0, :, 0], ahead(h, 0, right)))
             first[h][1].wait_recv()
             sbuf[n, h, prv, :, 1] = (ssum[n, h, prv, :, 1] + relay[n, h, 1].astype(F32)).astype(BF16)
-            first[h].append(send(sbuf.at[n, h, prv, :, 1], main.at[n, h, 1, :, 1], ahead(h, 0, left)))
+            first[h].append(send(sbuf.at[n, h, prv, :, 1], main.at[n, h, 2, :, 1], ahead(h, 0, left)))
         yield "relayed"
         second = []
         for h in halves:
-            for cp in first[h][2:]:
+            for cp in first[h][0 if n in STRAIGHT else 2:]:
                 cp.wait_recv()
             a, b = place(h)
-            total = ssum[n, h, a] + main[n, h, 0].astype(F32) + main[n, h, 1].astype(F32)
+            total = ssum[n, h, a] + main[n, h, 0].astype(F32) + main[n, h, 2].astype(F32)
+            if n in STRAIGHT:
+                total = total + main[n, h, 1].astype(F32)
             tsum[n, h] = total
             thalf[n, h] = total.astype(BF16)
             second.append([
@@ -336,6 +346,9 @@
                 cp.wait_recv()
         else:
             next(near if step == "n" else far)
+    for cp in started:
+        if all(cp is not back for back in returned):
+            cp.wait_send()
     for cp in returned:
         cp.wait_recv()
     got = rfin[...].astype(F32)
@@ -345,7 +358,7 @@
     mids1 = jnp.concatenate([mids[d] if MID_HALF[d] else empty for d in range(EXPERTS)], axis=0)
     got = jnp.concatenate([mains, mids0, mids1], axis=1).astype(BF16)
     out_ref[...] = nt(tn(placed, got), spread, lax.Precision.HIGHEST)
-    for cp in started:
+    for cp in returned:
         cp.wait_send()
 
 
@@ -380,7 +393,7 @@
                 pltpu.VMEM((2, 2, RING, RING, 2, packed, LANES), F32),
                 pltpu.VMEM((2, 2, RING, RING, 2, packed, LANES), BF16),
                 pltpu.VMEM((2, 2, 2, RING, packed, LANES), BF16),
-                pltpu.VMEM((2, 2, 2, RING, 2, packed, LANES), BF16),
+                pltpu.VMEM((2, 2, RING - 1, RING, 2, packed, LANES), BF16),
                 pltpu.VMEM((2, 2, RING, 2, packed, LANES), F32),
                 pltpu.VMEM((2, 2, RING, 2, packed, LANES), BF16),
                 pltpu.VMEM((2, 2, RING - 1, 2, packed, LANES), BF16),

time: 96.7 us -> 96 us (level)
  no operation moved by 1% of the time
where the time goes in v4:
time: 96 us; the launch traced here: 95.7 us
  Pallas kernels  94.4 us (98%)
  local copies, waits for them, and re-layouts  1.32 us (1%)
    pallas_call x1, Pallas kernels, local(): pl.pallas_call(kernel, out_shape=jax.ShapeDtypeStruct((tok, feat), F32),...  94.4 us

profile of v4, /device:TPU:6, one launch (start us, length us, event | category | flops | bytes accessed | tf_op | source)
XLA Modules:
  0.0 95.7 jit_solution(16460627435776758671)
XLA Ops:
  0.0 94.4 %shard_map.73 = f32[16,192]{1,0:T(8,128)} custom-call(bf16[16,192]{1,0:T(8,128)(2,1)} %tok_hbm.1, bf16[16,192]{1,0:T(8,128)(2,1)} %up_hbm.1, s32[2,16]{1,0:T(2,128)} %bitcast.2, f32[2,16]{1,0:T(2,128)} %bitcast.3, bf16[3072,128]{1,0:T(8,128)(2,1)} %wg_hbm.1, bf16[3072,128]{1,0:T(8,128)(2,1)} %wu_hbm.1, bf16[128,3072]{1,0:T(8,128)(2,1)} %wd_hbm.1), custom_call_target="tpu_custom_call" | custom-call | tf_op jit(solution)/shard_map/pallas_call | solution.py:375
  94.4 1.3 %copy.9 = f32[16,192]{1,0:T(8,128)} copy(f32[16,192]{1,0:T(8,128)} %shard_map.73) | data formatting | bytes 24576

commit v5 on v4

--- a/solution.py
+++ b/solution.py
@@ -67,7 +67,7 @@
         started.append(cp)
         return cp
 
-    partners = [at_dp((e + d) % EXPERTS * ZL + zl, core) for d in range(1, EXPERTS)]
+    partners = [at_dp((e + d) % EXPERTS * ZL + zl, core) for d in (4, 5, 3, 6, 2, 7, 1)]
     partners += [at_dp(z, 1 - core)]
     partners += [at_dp(e * ZL + (zl + d) % ZL, core) for d in range(1, ZL)]
     partners += [at_xy((x + d) % RING, y) for d in range(1, RING)]
@@ -86,19 +86,10 @@
     ]
     for cp in loads:
         cp.start()
-    for cp in loads[:4]:
-        cp.wait()
 
     slot = lax.broadcasted_iota(jnp.int32, (EXPERTS * cap, tok), 0)
     slot_e, slot_s = (e - (slot >> 3) + EXPERTS) & (EXPERTS - 1), slot & 7
-    ids = ids_ref[...]
-    one0 = jnp.where(ids[0:1, :] == slot_e, 1.0, 0.0).astype(F32)
-    one1 = jnp.where(ids[1:2, :] == slot_e, 1.0, 0.0).astype(F32)
     earlier = lax.broadcasted_iota(jnp.int32, (tok, tok), 0) < lax.broadcasted_iota(jnp.int32, (tok, tok), 1)
-    before = nn(one0 + one1, jnp.where(earlier, 1.0, 0.0).astype(F32))
-    fits = jnp.where(before == slot_s.astype(F32), 1.0, 0.0).astype(F32)
-    p0, p1 = one0 * fits, one1 * fits
-    placed = (p0 + p1).astype(BF16)
     rest = feat - LANES
     f = lax.broadcasted_iota(jnp.int32, (feat, 3 * LANES), 0)
     lane = lax.broadcasted_iota(jnp.int32, (feat, 3 * LANES), 1)
@@ -109,6 +100,15 @@
     to1 = even_also + odd * (odd_also - even_also)
     spread = jnp.where(lane == to0, 1.0, 0.0).astype(F32) + jnp.where(lane == to1, 1.0, 0.0).astype(F32)
     spread_half = spread.astype(BF16)
+    for cp in loads[:4]:
+        cp.wait()
+    ids = ids_ref[...]
+    one0 = jnp.where(ids[0:1, :] == slot_e, 1.0, 0.0).astype(F32)
+    one1 = jnp.where(ids[1:2, :] == slot_e, 1.0, 0.0).astype(F32)
+    before = nn(one0 + one1, jnp.where(earlier, 1.0, 0.0).astype(F32))
+    fits = jnp.where(before == slot_s.astype(F32), 1.0, 0.0).astype(F32)
+    p0, p1 = one0 * fits, one1 * fits
+    placed = (p0 + p1).astype(BF16)
     xw = nn(tok_ref[...], spread_half).astype(BF16)
     uw = nn(up_ref[...], spread_half).astype(BF16)
     rw = rw_ref[...]

time: 96 us -> 96.6 us (level)
  no operation moved by 1% of the time
where the time goes in v5:
time: 96.6 us; the launch traced here: 96.4 us
  Pallas kernels  95.1 us (98%)
  local copies, waits for them, and re-layouts  1.32 us (1%)
    pallas_call x1, Pallas kernels, local(): pl.pallas_call(kernel, out_shape=jax.ShapeDtypeStruct((tok, feat), F32),...  95.1 us

profile of v5, /device:TPU:6, one launch (start us, length us, event | category | flops | bytes accessed | tf_op | source)
XLA Modules:
  0.0 96.4 jit_solution(4132398394156354658)
XLA Ops:
  0.0 95.1 %shard_map.73 = f32[16,192]{1,0:T(8,128)} custom-call(bf16[16,192]{1,0:T(8,128)(2,1)} %tok_hbm.1, bf16[16,192]{1,0:T(8,128)(2,1)} %up_hbm.1, s32[2,16]{1,0:T(2,128)} %bitcast.2, f32[2,16]{1,0:T(2,128)} %bitcast.3, bf16[3072,128]{1,0:T(8,128)(2,1)} %wg_hbm.1, bf16[3072,128]{1,0:T(8,128)(2,1)} %wu_hbm.1, bf16[128,3072]{1,0:T(8,128)(2,1)} %wd_hbm.1), custom_call_target="tpu_custom_call" | custom-call | tf_op jit(solution)/shard_map/pallas_call | solution.py:375
  95.1 1.3 %copy.9 = f32[16,192]{1,0:T(8,128)} copy(f32[16,192]{1,0:T(8,128)} %shard_map.73) | data formatting | bytes 24576
